TPU v7x, 32 devices: a whole 2x2x4 slice. The times are simulated.
32 devices in a mesh: slab: 16 (over z, x, core), mem: 2 (over y).
Axes of the slice: x: 2, y: 2, z: 4, core: 2. Of those that a mesh axis runs over, the one named last changes fastest.
Arguments:
- anomalies: bfloat16 [16, 12, 512, 128], P('mem', None, 'slab'), may hold values from -6 to 6
- grad_in: float32 [12, 512, 128], P(None, 'slab'), may hold values from -6 to 6
- alpha: float32 [16, 12, 512, 128], P('mem', None, 'slab'), may hold values from -0.18 to 0.18
- land_sea: int32 [12, 512, 128], P(None, 'slab'), may hold values 0 or 1
- length_rates: float32 [2, 512, 128], P(None, 'slab'), may hold values from 0.125 to 0.25
- step_counts: int32 [2, 12], replicated, may hold values from 6 to 8, as said below
Outputs:
- direction: float32 [16, 12, 512, 128], P('mem', None, 'slab')
- grad_norm: float32 [], replicated
Inputs may be any that keep to these rules, and one draw needn't show every extreme that they name: `step_counts`: each level's number of transposed diffusion steps in each pass; in every draw some level takes 8 steps in both passes, and 6 is reached.
All inputs are finite; a program needn't handle non-finite values. No bound on the sum of `land_sea` on one device may be relied on, other than what follows from the above.
Results may differ from a plain program's by a relative error of at most 0.0003.
Values sent between devices are 32-bit elements; how exact they have to be, the bound alone decides.
A program may use at most 64 MiB of HBM per device.

v0:
```python
import functools

import jax
import jax.numpy as jnp
from jax import lax
from jax.experimental import pallas as pl
from jax.experimental.pallas import tpu as pltpu
from jax.sharding import PartitionSpec as P

NSTEP = 8
SURE = 6
W = NSTEP
SKEW = 2
MESH = pl.DeviceIdType.MESH


def kernel(
    ns, nm, count_all, members_all,
    cnt, anom, gin, land, rate, alpha_any, proj_any, stats,
    u0, u1, u2, hal, ohal, rhal, oc, coef, alpha, g, msum, mrecv, tsend, trecv,
    hsend, hrecv, csend, crecv, msend, mrecv_sem, tsend_sem, trecv_sem, loc_sem,
    out_sem,
):
    nmem, levels, nx, ny = anom.shape
    nall = ns * nm
    s = lax.axis_index("slab")
    q = lax.axis_index("mem")
    me = s * nm + q
    left = (lax.rem(s + ns - 1, ns), q)
    right = (lax.rem(s + 1, ns), q)

    def other(d):
        i = lax.rem(me + d, nall)
        return (lax.div(i, nm), lax.rem(i, nm))

    barrier = pltpu.get_barrier_semaphore()

    @pl.loop(1, nall)
    def _(d):
        pl.semaphore_signal(barrier, inc=1, device_id=other(d), device_id_type=MESH)

    acopy = pltpu.make_async_copy(alpha_any, alpha, loc_sem)
    acopy.start()
    pl.semaphore_wait(barrier, nall - 1)

    def rdma(src, dst, ss, rs, dev):
        return pltpu.make_async_remote_copy(
            src_ref=src, dst_ref=dst, send_sem=ss, recv_sem=rs, device_id=dev,
            device_id_type=MESH,
        )

    def coef_copies():
        res = []
        for side, lo, dev in ((1, 0, left), (0, nx - W, right)):
            res.append(rdma(land.at[:, pl.ds(lo, W), :], ohal.at[side],
                            csend.at[0, side], crecv.at[0, side], dev))
            res.append(rdma(rate.at[:, pl.ds(lo, W), :], rhal.at[side],
                            csend.at[1, side], crecv.at[1, side], dev))
        return res

    def halo_copies(u, p, l):
        rows = W * nmem
        return [
            rdma(u.at[l, pl.ds(lo, rows), :], hal.at[p, side, l],
                 hsend.at[p, side, l], hrecv.at[p, side, l], dev)
            for side, lo, dev in ((1, 0, left), (0, nx * nmem - rows, right))
        ]

    def mean_copies(l):
        return [
            rdma(msum.at[l], mrecv.at[k - 1, l], msend.at[k - 1, l],
                 mrecv_sem.at[k - 1, l], (s, lax.rem(q + k, nm)))
            for k in range(1, nm)
        ]

    def out_copy(l):
        return pltpu.make_async_copy(g.at[:, l], proj_any.at[:, l], out_sem.at[l])

    for c in coef_copies():
        c.start()

    @pl.loop(0, levels)
    def _(l):
        for h in range(nx // 16):
            facs = []
            for t in (2 * h, 2 * h + 1):
                sl = pl.ds(8 * t, 8)
                facs.append(gin[l, sl, :] * (rate[1, sl, :] * land[l, sl, :].astype(jnp.float32)))
            for m in range(nmem):
                a = anom[m, l, pl.ds(16 * h, 16), :].astype(jnp.float32)
                for j in range(2):
                    u0[l, pl.ds((16 * h + 8 * j) * nmem + m, 8, stride=nmem), :] = (
                        a[8 * j:8 * j + 8] * facs[j]
                    )
        for c in halo_copies(u0, 0, l):
            c.start()

    for c in coef_copies():
        c.wait()

    lane = lax.broadcasted_iota(jnp.int32, (8, ny), 1)
    not_first = lane > 0
    not_last = lane < ny - 1

    def sides(v):
        return (jnp.where(not_first, pltpu.roll(v, 1, 1), 0.0)
                + jnp.where(not_last, pltpu.roll(v, ny - 1, 1), 0.0))

    ext = nx + 2 * W
    zero = jnp.zeros((8, ny), jnp.float32)
    oc[pl.ds(0, 8), :] = zero
    oc[pl.ds(8 + ext, 8), :] = zero

    def rates_at(p, t):
        if t == 0:
            return rhal[0, p]
        if t == ext // 8 - 1:
            return rhal[1, p]
        return rate[p, pl.ds(8 * t - W, 8), :]

    def make_coefs(l):
        oc[pl.ds(8, 8), :] = ohal[0, l].astype(jnp.float32)
        for t in range(nx // 8):
            oc[pl.ds(8 + W + 8 * t, 8), :] = land[l, pl.ds(8 * t, 8), :].astype(jnp.float32)
        oc[pl.ds(8 + W + nx, 8), :] = ohal[1, l].astype(jnp.float32)
        for t in range(ext // 8):
            o = oc[pl.ds(8 + 8 * t, 8), :]
            around = oc[pl.ds(7 + 8 * t, 8), :] + oc[pl.ds(9 + 8 * t, 8), :] + sides(o)
            for p in (1, 0):
                k = o * rates_at(p, t)
                coef[p, 0, l, pl.ds(8 * t, 8), :] = k
                coef[p, 1, l, pl.ds(8 * t, 8), :] = 1.0 - k * around

    def wide(row):
        return jnp.broadcast_to(row, (nmem, ny))

    def run(order, p, l, src, put):
        steps = jnp.full((nmem, ny), cnt[p, l], jnp.int32)
        masks = {t: steps >= t for t in range(SURE + 1, NSTEP + 1)}
        vals = [{} for _ in range(NSTEP + 1)]
        for d in range(-W, nx + W + SKEW * NSTEP + 1):
            if d < nx + W:
                if d < 0:
                    v = hal[order, 0, l, pl.ds((d + W) * nmem, nmem), :]
                elif d < nx:
                    v = src[l, pl.ds(d * nmem, nmem), :]
                else:
                    v = hal[order, 1, l, pl.ds((d - nx) * nmem, nmem), :]
                vals[0][d] = v
            for t in range(1, NSTEP + 1):
                x = d - SKEW * t
                if not -(W - t) <= x <= nx - 1 + W - t:
                    continue
                old = vals[t - 1]
                v = old[x]
                k = wide(coef[p, 0, l, pl.ds(x + W, 1), :])
                a = wide(coef[p, 1, l, pl.ds(x + W, 1), :])
                new = a * v + k * ((old[x - 1] + old[x + 1]) + sides(v))
                if t > SURE:
                    new = jnp.where(masks[t], new, v)
                if t == NSTEP:
                    put(x, new)
                else:
                    vals[t][x] = new

    @pl.loop(0, levels)
    def _(l):
        make_coefs(l)
        for c in halo_copies(u0, 0, l):
            c.wait_recv()

        def put(x, v):
            ratio = rate[0, pl.ds(x, 1), :] / rate[1, pl.ds(x, 1), :]
            u1[l, pl.ds(x * nmem, nmem), :] = v * wide(ratio)

        run(0, 1, l, u0, put)
        for c in halo_copies(u1, 1, l):
            c.start()

    acopy.wait()

    @pl.loop(0, levels)
    def _(l):
        for c in halo_copies(u1, 1, l):
            c.wait_recv()

        def put(x, v):
            u2[pl.ds(x * nmem, nmem), :] = v

        run(1, 0, l, u1, put)
        for h in range(nx // 16):
            cs = []
            for t in (2 * h, 2 * h + 1):
                sl = pl.ds(8 * t, 8)
                cs.append((gin[l, sl, :], land[l, sl, :] > 0, 1.0 / rate[0, sl, :]))
            tot = [zero, zero]
            for m in range(nmem):
                a = anom[m, l, pl.ds(16 * h, 16), :].astype(jnp.float32)
                for j in range(2):
                    gi, wet, inv = cs[j]
                    x = 16 * h + 8 * j
                    u = u2[pl.ds(x * nmem + m, 8, stride=nmem), :]
                    v = alpha[m, l, pl.ds(x, 8), :] + jnp.where(wet, u * inv, a[8 * j:8 * j + 8] * gi)
                    g[m, l, pl.ds(x, 8), :] = v
                    tot[j] = tot[j] + v
            for j in range(2):
                msum[l, pl.ds(16 * h + 8 * j, 8), :] = tot[j]
        for c in mean_copies(l):
            c.start()

    def project(l, acc):
        for c in mean_copies(l):
            c.wait_recv()
        acc = list(acc)
        for t in range(nx // 8):
            sl = pl.ds(8 * t, 8)
            mean = msum[l, sl, :]
            for k in range(nm - 1):
                mean = mean + mrecv[k, l, sl, :]
            mean = mean * (1.0 / members_all)
            for m in range(nmem):
                v = g[m, l, sl, :] - mean
                g[m, l, sl, :] = v
                acc[m % 4] = acc[m % 4] + v * v
        out_copy(l).start()
        return tuple(acc)

    acc = lax.fori_loop(0, levels, project, (zero,) * 4)
    own = (acc[0] + acc[1]) + (acc[2] + acc[3])
    tsend[...] = own

    def total_copy(d):
        return rdma(tsend, trecv.at[d], tsend_sem.at[d], trecv_sem.at[d], other(d))

    @pl.loop(1, nall)
    def _(d):
        total_copy(d).start()

    @pl.loop(0, levels)
    def _(l):
        for p, u in ((0, u0), (1, u1)):
            for c in halo_copies(u, p, l):
                c.wait_send()
        for c in mean_copies(l):
            c.wait_send()
        out_copy(l).wait()

    trecv[0] = own

    @pl.loop(1, nall)
    def _(d):
        total_copy(d).wait()

    def add(i, a):
        return a + trecv[lax.rem(me - i + nall, nall)]

    whole = lax.fori_loop(0, nall, add, zero)
    total = jnp.full((8, ny), jnp.sum(whole), jnp.float32)
    stats[0] = jnp.sqrt(total)
    stats[1] = 1.0 / jnp.sqrt(total * (1.0 / count_all) + 1e-6)


def on_device(anomalies, grad_in, alpha, land_sea, length_rates, step_counts):
    nmem, levels, nx, ny = anomalies.shape
    ns, nm = lax.axis_size("slab"), lax.axis_size("mem")
    nall = ns * nm
    members_all = nmem * nm
    count_all = members_all * levels * nx * ns * ny
    f32 = jnp.float32
    vm = pl.BlockSpec(memory_space=pltpu.VMEM)
    dma = pltpu.SemaphoreType.DMA
    body = functools.partial(kernel, ns, nm, count_all, members_all)
    projected, stats = pl.pallas_call(
        body,
        out_shape=(
            jax.ShapeDtypeStruct(alpha.shape, f32),
            jax.ShapeDtypeStruct((2, 8, ny), f32),
        ),
        in_specs=[pl.BlockSpec(memory_space=pltpu.SMEM), vm, vm, vm, vm,
                  pl.BlockSpec(memory_space=pl.ANY)],
        out_specs=(pl.BlockSpec(memory_space=pl.ANY), vm),
        scratch_shapes=[
            pltpu.VMEM((levels, nx * nmem, ny), f32),
            pltpu.VMEM((levels, nx * nmem, ny), f32),
            pltpu.VMEM((nx * nmem, ny), f32),
            pltpu.VMEM((2, 2, levels, W * nmem, ny), f32),
            pltpu.VMEM((2, levels, W, ny), jnp.int32),
            pltpu.VMEM((2, 2, W, ny), f32),
            pltpu.VMEM((nx + 2 * W + 16, ny), f32),
            pltpu.VMEM((2, 2, levels, nx + 2 * W, ny), f32),
            pltpu.VMEM(alpha.shape, f32),
            pltpu.VMEM(alpha.shape, f32),
            pltpu.VMEM((levels, nx, ny), f32),
            pltpu.VMEM((max(nm - 1, 1), levels, nx, ny), f32),
            pltpu.VMEM((8, ny), f32),
            pltpu.VMEM((nall, 8, ny), f32),
            dma((2, 2, levels)), dma((2, 2, levels)),
            dma((2, 2)), dma((2, 2)),
            dma((max(nm - 1, 1), levels)), dma((max(nm - 1, 1), levels)),
            dma((nall,)), dma((nall,)),
            dma, dma((levels,)),
        ],
        compiler_params=pltpu.CompilerParams(
            collective_id=0, has_side_effects=True, vmem_limit_bytes=48 * 2**20
        ),
    )(step_counts, anomalies, grad_in, land_sea, length_rates, alpha)
    return (projected * stats[1, 0, 0], stats[0, 0, 0])


def solution(mesh):
    in_specs = (
        P("mem", None, "slab", None),
        P(None, "slab", None),
        P("mem", None, "slab", None),
        P(None, "slab", None),
        P(None, "slab", None),
        P(),
    )
    out_specs = (P("mem", None, "slab", None), P())
    return jax.shard_map(
        on_device, mesh=mesh, in_specs=in_specs, out_specs=out_specs, check_vma=False
    )
```

profile of v0, /device:TPU:0, one launch (start us, length us, event | category | flops | bytes accessed | tf_op | source)
XLA Modules:
  0.0 63.1 jit_solution(3892233682881718319)
XLA Ops:
  0.6 0.0 copy-start
  0.6 1.4 %copy-done = f32[8,12,32,128]{3,2,1,0:T(8,128)S(1)} copy-done((f32[8,12,32,128]{3,2,1,0:T(8,128)S(1)}, f32[8,12,32,128]{3,2,1,0:T(8,128)}, u32[]{:S(2)}) %copy-start) | copy-done | bytes 1572888
  2.0 0.0 copy-start.1
  2.0 1.1 %copy-done.1 = bf16[8,12,32,128]{3,2,1,0:T(8,128)(2,1)S(1)} copy-done((bf16[8,12,32,128]{3,2,1,0:T(8,128)(2,1)S(1)}, bf16[8,12,32,128]{3,2,1,0:T(8,128)(2,1)}, u32[]{:S(2)}) %copy-start.1) | copy-done | bytes 786456
  3.2 0.0 copy-start.2
  3.2 0.9 %copy-done.2 = f32[12,32,128]{2,1,0:T(8,128)S(1)} copy-done((f32[12,32,128]{2,1,0:T(8,128)S(1)}, f32[12,32,128]{2,1,0:T(8,128)}, u32[]{:S(2)}) %copy-start.2) | copy-done | bytes 196632
  4.1 0.0 copy-start.3
  4.1 0.9 %copy-done.3 = s32[12,32,128]{2,1,0:T(8,128)S(1)} copy-done((s32[12,32,128]{2,1,0:T(8,128)S(1)}, s32[12,32,128]{2,1,0:T(8,128)}, u32[]{:S(2)}) %copy-start.3) | copy-done | bytes 196632
  5.0 0.0 copy-start.4
  5.0 0.8 %copy-done.4 = f32[2,32,128]{2,1,0:T(8,128)S(1)} copy-done((f32[2,32,128]{2,1,0:T(8,128)S(1)}, f32[2,32,128]{2,1,0:T(8,128)}, u32[]{:S(2)}) %copy-start.4) | copy-done | bytes 32792
  5.8 0.0 copy-start.5
  5.8 0.7 %copy-done.5 = s32[2,12]{1,0:T(2,128)S(1)} copy-done((s32[2,12]{1,0:T(2,128)S(1)}, s32[2,12]{1,0:T(2,128)}, u32[]{:S(2)}) %copy-start.5) | copy-done | bytes 120
  6.5 54.2 %shard_map.77 = (f32[8,12,32,128]{3,2,1,0:T(8,128)S(1)}, f32[2,8,128]{2,1,0:T(8,128)S(1)}) custom-call(s32[2,12]{1,0:T(2,128)S(1)} %copy-done.5, bf16[8,12,32,128]{3,2,1,0:T(8,128)(2,1)S(1)} %copy-done.1, f32[12,32,128]{2,1,0:T(8,128)S(1)} %copy-done.2, s32[12,32,128]{2,1,0:T(8,128)S(1)} %copy-done.3, f32[2,32,128]{2,1,0:T(8,128)S(1)} %copy-done.4, ...), custom_call_target="tpu_custom_call" | custom-call | tf_op jit(solution)/shard_map/pallas_call | solution.py:273
  60.7 0.5 fusion
  61.2 1.9 %broadcast_multiply_fusion = f32[8,12,32,128]{3,2,1,0:T(8,128)} fusion(f32[8,12,32,128]{3,2,1,0:T(8,128)S(1)} %get-tuple-element.4, f32[]{:T(128)} %bitcast), kind=kLoop, calls=%fused_computation | loop fusion | flops 393216 | bytes 3145732 | tf_op jit(solution)/shard_map/mul | solution.py:307
Async XLA Ops:
  0.6 1.4 %copy-start = (f32[8,12,32,128]{3,2,1,0:T(8,128)S(1)}, f32[8,12,32,128]{3,2,1,0:T(8,128)}, u32[]{:S(2)}) copy-start(f32[8,12,32,128]{3,2,1,0:T(8,128)} %alpha_any.1) | copy-start | bytes 4718596
  2.0 1.1 %copy-start.1 = (bf16[8,12,32,128]{3,2,1,0:T(8,128)(2,1)S(1)}, bf16[8,12,32,128]{3,2,1,0:T(8,128)(2,1)}, u32[]{:S(2)}) copy-start(bf16[8,12,32,128]{3,2,1,0:T(8,128)(2,1)} %anom.1) | copy-start | bytes 2359300
  3.2 0.9 %copy-start.2 = (f32[12,32,128]{2,1,0:T(8,128)S(1)}, f32[12,32,128]{2,1,0:T(8,128)}, u32[]{:S(2)}) copy-start(f32[12,32,128]{2,1,0:T(8,128)} %gin.1) | copy-start | bytes 589828
  4.1 0.9 %copy-start.3 = (s32[12,32,128]{2,1,0:T(8,128)S(1)}, s32[12,32,128]{2,1,0:T(8,128)}, u32[]{:S(2)}) copy-start(s32[12,32,128]{2,1,0:T(8,128)} %land.1) | copy-start | bytes 589828
  5.0 0.8 %copy-start.4 = (f32[2,32,128]{2,1,0:T(8,128)S(1)}, f32[2,32,128]{2,1,0:T(8,128)}, u32[]{:S(2)}) copy-start(f32[2,32,128]{2,1,0:T(8,128)} %rate.1) | copy-start | bytes 98308
  5.8 0.7 %copy-start.5 = (s32[2,12]{1,0:T(2,128)S(1)}, s32[2,12]{1,0:T(2,128)}, u32[]{:S(2)}) copy-start(s32[2,12]{1,0:T(2,128)} %cnt.1) | copy-start | bytes 292
where the time goes:
time: 63.4 us; the launch traced here: 63.1 us
  Pallas kernels  54.2 us (85%)
  local copies, waits for them, and re-layouts  6.34 us (10%)
  other arithmetic  1.87 us (3%)
  between operations  0.65 us (1%)
    pallas_call x1, Pallas kernels, on_device(): pl.pallas_call(body, out_shape=(jax.ShapeDtypeStruct(alpha.shape, f32), j...  54.2 us
    unnamed x12, local copies, waits for them, and re-layouts  5.82 us
    mul x1, other arithmetic, on_device(): return (projected * stats[1, 0, 0], stats[0, 0, 0])  1.87 us

commit v1 on v0

v1 whole, which is shorter than its diff:
```python
import functools

import jax
import jax.numpy as jnp
from jax import lax
from jax.experimental import pallas as pl
from jax.experimental.pallas import tpu as pltpu
from jax.sharding import PartitionSpec as P

NSTEP = 8
SURE = 6
W = NSTEP
GROUP = 3
MESH = pl.DeviceIdType.MESH


def kernel(
    ns, nm, count_all, members_all,
    cnt_any, anom_any, gin_any, land_any, rate_any, alpha_any, proj_any, stats,
    cnt, anom, gin, land, rate, bk, ba, tri, ratio, u0, u1, u2, hal, ohal, rhal, oc, coef, alpha, g, sums, mean_all, tsend, trecv,
    hsend, hrecv, csend, crecv, msend, mrecv_sem, tsend_sem, trecv_sem, loc_sem,
    out_sem,
):
    nmem, levels, nx, ny = anom.shape
    s = lax.axis_index("slab")
    q = lax.axis_index("mem")
    left = (lax.rem(s + ns - 1, ns), q)
    right = (lax.rem(s + 1, ns), q)

    def along(d):
        return (lax.rem(s + d, ns), q)

    barrier = pltpu.get_barrier_semaphore()

    for d in range(1, ns):
        pl.semaphore_signal(barrier, inc=1, device_id=along(d), device_id_type=MESH)
    for d in range(1, nm):
        pl.semaphore_signal(barrier, inc=1, device_id=(s, lax.rem(q + d, nm)),
                            device_id_type=MESH)

    loads = [
        pltpu.make_async_copy(src, dst, loc_sem.at[i])
        for i, (src, dst) in enumerate((
            (land_any, land), (rate_any, rate), (gin_any, gin), (anom_any, anom),
            (cnt_any, cnt), (alpha_any, alpha)))
    ]
    for c in loads:
        c.start()
    loads[0].wait()
    loads[1].wait()
    pl.semaphore_wait(barrier, ns + nm - 2)

    def rdma(src, dst, ss, rs, dev):
        return pltpu.make_async_remote_copy(
            src_ref=src, dst_ref=dst, send_sem=ss, recv_sem=rs, device_id=dev,
            device_id_type=MESH,
        )

    def coef_copies():
        res = []
        for side, lo, dev in ((1, 0, left), (0, nx - W, right)):
            res.append(rdma(land.at[:, pl.ds(lo, W), :], ohal.at[side],
                            csend.at[0, side], crecv.at[0, side], dev))
            res.append(rdma(rate.at[:, pl.ds(lo, W), :], rhal.at[side],
                            csend.at[1, side], crecv.at[1, side], dev))
        return res

    def halo_copies(u, p, l):
        rows = W * nmem
        return [
            rdma(u.at[l, pl.ds(lo, rows), :], hal.at[p, side, l],
                 hsend.at[p, side, l], hrecv.at[p, side, l], dev)
            for side, lo, dev in ((1, 0, left), (0, nx * nmem - rows, right))
        ]

    def mean_copies(l):
        return [
            rdma(sums.at[0, l], sums.at[k, l], msend.at[k - 1, l],
                 mrecv_sem.at[k - 1, l], (s, lax.rem(q + k, nm)))
            for k in range(1, nm)
        ]

    def out_copy(l):
        return pltpu.make_async_copy(g.at[:, l], proj_any.at[:, l], out_sem.at[l])

    for c in coef_copies():
        c.start()
    loads[2].wait()
    loads[3].wait()

    @pl.loop(0, levels)
    def _(l):
        for h in range(nx // 16):
            facs = []
            for t in (2 * h, 2 * h + 1):
                sl = pl.ds(8 * t, 8)
                facs.append(gin[l, sl, :] * (rate[1, sl, :] * land[l, sl, :].astype(jnp.float32)))
            for m in range(nmem):
                a = anom[m, l, pl.ds(16 * h, 16), :].astype(jnp.float32)
                for j in range(2):
                    u0[l, pl.ds((16 * h + 8 * j) * nmem + m, 8, stride=nmem), :] = (
                        a[8 * j:8 * j + 8] * facs[j]
                    )
        for c in halo_copies(u0, 0, l):
            c.start()

    for c in coef_copies():
        c.wait()
    loads[4].wait()

    lane = lax.broadcasted_iota(jnp.int32, (8, ny), 1)
    not_first = lane > 0
    not_last = lane < ny - 1

    def sides(v):
        return (jnp.where(not_first, pltpu.roll(v, 1, 1), 0.0)
                + jnp.where(not_last, pltpu.roll(v, ny - 1, 1), 0.0))

    ext = nx + 2 * W
    zero = jnp.zeros((8, ny), jnp.float32)
    oc[pl.ds(0, 8), :] = zero
    oc[pl.ds(8 + ext, 8), :] = zero

    def rates_at(p, t):
        if t == 0:
            return rhal[0, p]
        if t == ext // 8 - 1:
            return rhal[1, p]
        return rate[p, pl.ds(8 * t - W, 8), :]

    ratio[...] = rate[0] / rate[1]

    def make_coefs(l):
        oc[pl.ds(8, 8), :] = ohal[0, l].astype(jnp.float32)
        for t in range(nx // 8):
            oc[pl.ds(8 + W + 8 * t, 8), :] = land[l, pl.ds(8 * t, 8), :].astype(jnp.float32)
        oc[pl.ds(8 + W + nx, 8), :] = ohal[1, l].astype(jnp.float32)
        for t in range(ext // 8):
            o = oc[pl.ds(8 + 8 * t, 8), :]
            around = oc[pl.ds(7 + 8 * t, 8), :] + oc[pl.ds(9 + 8 * t, 8), :] + sides(o)
            for p in (1, 0):
                k = o * rates_at(p, t)
                coef[p, 0, l, pl.ds(8 * t, 8), :] = k
                coef[p, 1, l, pl.ds(8 * t, 8), :] = 1.0 - k * around

    def wide(row):
        return jnp.broadcast_to(row, (nmem, ny))

    i = lax.broadcasted_iota(jnp.int32, (ny, ny), 0)
    j = lax.broadcasted_iota(jnp.int32, (ny, ny), 1)
    near = jnp.where(jnp.abs(i - j) == 1, 1.0, 0.0).astype(jnp.bfloat16)
    tri[pl.ds(0, ny), :] = near
    tri[pl.ds(ny, ny), :] = near

    def run(order, p, ls, src, put):
        masks, fields = [], []
        for n, l in enumerate(ls):
            steps = jnp.full((nmem, ny), cnt[p, l], jnp.int32)
            masks.append({t: steps >= t for t in range(SURE + 1, NSTEP + 1)})
            for x in range(1, ext - 1):
                bk[n, pl.ds(x * nmem, nmem), :] = wide(coef[p, 0, l, pl.ds(x, 1), :])
                ba[n, pl.ds(x * nmem, nmem), :] = wide(coef[p, 1, l, pl.ds(x, 1), :])
            fields.append(jnp.concatenate(
                [hal[order, 0, l], src[l], hal[order, 1, l]], axis=0))
        for t in range(1, NSTEP + 1):
            mids = [u[nmem:-nmem] for u in fields]
            rows = mids[0].shape[0]
            mid = jnp.concatenate(mids, axis=0)
            high = mid.astype(jnp.bfloat16)
            low = (mid - high.astype(jnp.float32)).astype(jnp.bfloat16)
            both = jnp.dot(jnp.concatenate([high, low], axis=1), tri[...],
                           preferred_element_type=jnp.float32)
            for n, u in enumerate(fields):
                at = pl.ds(t * nmem, rows)
                side = both[n * rows:(n + 1) * rows]
                new = ba[n, at, :] * mids[n] + bk[n, at, :] * (
                    (u[:-2 * nmem] + u[2 * nmem:]) + side)
                if t > SURE:
                    mask = masks[n][t]
                    new = jnp.concatenate(
                        [jnp.where(mask, new[x:x + nmem], mids[n][x:x + nmem])
                         for x in range(0, rows, nmem)], axis=0)
                fields[n] = new
        for n, l in enumerate(ls):
            for x in range(nx):
                put(n, l, x, fields[n][x * nmem:(x + 1) * nmem])

    @pl.loop(0, levels // GROUP)
    def _(b):
        ls = [b * GROUP + n for n in range(GROUP)]
        for l in ls:
            make_coefs(l)
            for c in halo_copies(u0, 0, l):
                c.wait_recv()

        def put(n, l, x, v):
            u1[l, pl.ds(x * nmem, nmem), :] = v * wide(ratio[pl.ds(x, 1), :])

        run(0, 1, ls, u0, put)
        for l in ls:
            for c in halo_copies(u1, 1, l):
                c.start()

    loads[5].wait()

    @pl.loop(0, levels // GROUP)
    def _(b):
        ls = [b * GROUP + n for n in range(GROUP)]
        for l in ls:
            for c in halo_copies(u1, 1, l):
                c.wait_recv()

        def put(n, l, x, v):
            u2[n, pl.ds(x * nmem, nmem), :] = v

        run(1, 0, ls, u1, put)
        for n, l in enumerate(ls):
            spread = zero
            for h in range(nx // 16):
                cs = []
                for t in (2 * h, 2 * h + 1):
                    sl = pl.ds(8 * t, 8)
                    cs.append((gin[l, sl, :], land[l, sl, :] > 0, 1.0 / rate[0, sl, :]))
                tot = [zero, zero]
                kept = [[], []]
                for m in range(nmem):
                    a = anom[m, l, pl.ds(16 * h, 16), :].astype(jnp.float32)
                    for j in range(2):
                        gi, wet, inv = cs[j]
                        x = 16 * h + 8 * j
                        u = u2[n, pl.ds(x * nmem + m, 8, stride=nmem), :]
                        v = alpha[m, l, pl.ds(x, 8), :] + jnp.where(wet, u * inv, a[8 * j:8 * j + 8] * gi)
                        g[m, l, pl.ds(x, 8), :] = v
                        tot[j] = tot[j] + v
                        kept[j].append(v)
                for j in range(2):
                    sums[0, l, pl.ds(16 * h + 8 * j, 8), :] = tot[j]
                    here = tot[j] * (1.0 / nmem)
                    for v in kept[j]:
                        spread = spread + (v - here) * (v - here)
            sums[0, l, pl.ds(nx, 8), :] = spread
            for c in mean_copies(l):
                c.start()

    order = [lax.rem(q - i + nm, nm) for i in range(nm)]

    def square(l, acc):
        for c in mean_copies(l):
            c.wait_recv()
        end = pl.ds(nx, 8)
        for k in order:
            acc = acc + sums[k, l, end, :]
        for t in range(nx // 8):
            sl = pl.ds(8 * t, 8)
            parts = [sums[k, l, sl, :] for k in order]
            mean = parts[0]
            for v in parts[1:]:
                mean = mean + v
            mean = mean * (1.0 / members_all)
            mean_all[l, sl, :] = mean
            for v in parts:
                gap = v * (1.0 / nmem) - mean
                acc = acc + nmem * (gap * gap)
        return acc

    own = lax.fori_loop(0, levels, square, zero)
    tsend[...] = own

    def total_copy(d):
        return rdma(tsend, trecv.at[d], tsend_sem.at[d], trecv_sem.at[d], along(d))

    for d in range(1, ns):
        total_copy(d).start()

    @pl.loop(0, levels)
    def _(l):
        for t in range(nx // 8):
            sl = pl.ds(8 * t, 8)
            mean = mean_all[l, sl, :]
            for m in range(nmem):
                g[m, l, sl, :] = g[m, l, sl, :] - mean
        out_copy(l).start()

    @pl.loop(0, levels)
    def _(l):
        for p, u in ((0, u0), (1, u1)):
            for c in halo_copies(u, p, l):
                c.wait_send()
        for c in mean_copies(l):
            c.wait_send()

    trecv[0] = own
    for d in range(1, ns):
        total_copy(d).wait()

    whole = zero
    for i in range(ns):
        whole = whole + trecv[lax.rem(s - i + ns, ns)]
    total = jnp.full((8, ny), jnp.sum(whole), jnp.float32)
    stats[0] = jnp.sqrt(total)
    stats[1] = 1.0 / jnp.sqrt(total * (1.0 / count_all) + 1e-6)

    @pl.loop(0, levels)
    def _(l):
        out_copy(l).wait()


def on_device(anomalies, grad_in, alpha, land_sea, length_rates, step_counts):
    nmem, levels, nx, ny = anomalies.shape
    ns, nm = lax.axis_size("slab"), lax.axis_size("mem")
    members_all = nmem * nm
    count_all = members_all * levels * nx * ns * ny
    f32 = jnp.float32
    vm = pl.BlockSpec(memory_space=pltpu.VMEM)
    dma = pltpu.SemaphoreType.DMA
    body = functools.partial(kernel, ns, nm, count_all, members_all)
    projected, stats = pl.pallas_call(
        body,
        out_shape=(
            jax.ShapeDtypeStruct(alpha.shape, f32),
            jax.ShapeDtypeStruct((2, 8, ny), f32),
        ),
        in_specs=[pl.BlockSpec(memory_space=pl.ANY)] * 6,
        out_specs=(pl.BlockSpec(memory_space=pl.ANY), vm),
        scratch_shapes=[
            pltpu.SMEM(step_counts.shape, jnp.int32),
            pltpu.VMEM(anomalies.shape, anomalies.dtype),
            pltpu.VMEM(grad_in.shape, f32),
            pltpu.VMEM(land_sea.shape, jnp.int32),
            pltpu.VMEM(length_rates.shape, f32),
            pltpu.VMEM((GROUP, (nx + 2 * W) * nmem, ny), f32),
            pltpu.VMEM((GROUP, (nx + 2 * W) * nmem, ny), f32),
            pltpu.VMEM((2 * ny, ny), jnp.bfloat16),
            pltpu.VMEM((nx, ny), f32),
            pltpu.VMEM((levels, nx * nmem, ny), f32),
            pltpu.VMEM((levels, nx * nmem, ny), f32),
            pltpu.VMEM((GROUP, nx * nmem, ny), f32),
            pltpu.VMEM((2, 2, levels, W * nmem, ny), f32),
            pltpu.VMEM((2, levels, W, ny), jnp.int32),
            pltpu.VMEM((2, 2, W, ny), f32),
            pltpu.VMEM((nx + 2 * W + 16, ny), f32),
            pltpu.VMEM((2, 2, levels, nx + 2 * W, ny), f32),
            pltpu.VMEM(alpha.shape, f32),
            pltpu.VMEM(alpha.shape, f32),
            pltpu.VMEM((nm, levels, nx + 8, ny), f32),
            pltpu.VMEM((levels, nx, ny), f32),
            pltpu.VMEM((8, ny), f32),
            pltpu.VMEM((ns, 8, ny), f32),
            dma((2, 2, levels)), dma((2, 2, levels)),
            dma((2, 2)), dma((2, 2)),
            dma((max(nm - 1, 1), levels)), dma((max(nm - 1, 1), levels)),
            dma((ns,)), dma((ns,)),
            dma((6,)), dma((levels,)),
        ],
        compiler_params=pltpu.CompilerParams(
            collective_id=0, has_side_effects=True, vmem_limit_bytes=48 * 2**20
        ),
    )(step_counts, anomalies, grad_in, land_sea, length_rates, alpha)
    return (projected * stats[1, 0, 0], stats[0, 0, 0])


def solution(mesh):
    in_specs = (
        P("mem", None, "slab", None),
        P(None, "slab", None),
        P("mem", None, "slab", None),
        P(None, "slab", None),
        P(None, "slab", None),
        P(),
    )
    out_specs = (P("mem", None, "slab", None), P())
    return jax.shard_map(
        on_device, mesh=mesh, in_specs=in_specs, out_specs=out_specs, check_vma=False
    )
```

time: 63.4 us -> 48.6 us (0.77)
  Pallas kernels: 54.2 us -> 39.4 us
    pallas_call x1, Pallas kernels: 54.2 us -> 39.4 us  [on_device(): pl.pallas_call(body, out_shape=(jax.ShapeDtypeStruct(alpha.shape, f32), j...]
where the time goes in v1:
time: 48.6 us; the launch traced here: 48.2 us
  Pallas kernels  39.4 us (81%)
  local copies, waits for them, and re-layouts  6.34 us (13%)
  other arithmetic  1.87 us (4%)
  between operations  0.65 us (1%)
    pallas_call x1, Pallas kernels, on_device(): pl.pallas_call(body, out_shape=(jax.ShapeDtypeStruct(alpha.shape, f32), j...  39.4 us
    unnamed x12, local copies, waits for them, and re-layouts  5.82 us
    mul x1, other arithmetic, on_device(): return (projected * stats[1, 0, 0], stats[0, 0, 0])  1.87 us

profile of v1, /device:TPU:0, one launch (start us, length us, event | category | flops | bytes accessed | tf_op | source)
XLA Modules:
  0.0 48.2 jit_solution(14964058781607465263)
XLA Ops:
  0.6 0.0 copy-start
  0.6 1.4 %copy-done = f32[8,12,32,128]{3,2,1,0:T(8,128)S(1)} copy-done((f32[8,12,32,128]{3,2,1,0:T(8,128)S(1)}, f32[8,12,32,128]{3,2,1,0:T(8,128)}, u32[]{:S(2)}) %copy-start) | copy-done | bytes 1572888
  2.0 0.0 copy-start.1
  2.0 1.1 %copy-done.1 = bf16[8,12,32,128]{3,2,1,0:T(8,128)(2,1)S(1)} copy-done((bf16[8,12,32,128]{3,2,1,0:T(8,128)(2,1)S(1)}, bf16[8,12,32,128]{3,2,1,0:T(8,128)(2,1)}, u32[]{:S(2)}) %copy-start.1) | copy-done | bytes 786456
  3.2 0.0 copy-start.2
  3.2 0.9 %copy-done.2 = f32[12,32,128]{2,1,0:T(8,128)S(1)} copy-done((f32[12,32,128]{2,1,0:T(8,128)S(1)}, f32[12,32,128]{2,1,0:T(8,128)}, u32[]{:S(2)}) %copy-start.2) | copy-done | bytes 196632
  4.1 0.0 copy-start.3
  4.1 0.9 %copy-done.3 = s32[12,32,128]{2,1,0:T(8,128)S(1)} copy-done((s32[12,32,128]{2,1,0:T(8,128)S(1)}, s32[12,32,128]{2,1,0:T(8,128)}, u32[]{:S(2)}) %copy-start.3) | copy-done | bytes 196632
  5.0 0.0 copy-start.4
  5.0 0.8 %copy-done.4 = f32[2,32,128]{2,1,0:T(8,128)S(1)} copy-done((f32[2,32,128]{2,1,0:T(8,128)S(1)}, f32[2,32,128]{2,1,0:T(8,128)}, u32[]{:S(2)}) %copy-start.4) | copy-done | bytes 32792
  5.8 0.0 copy-start.5
  5.8 0.7 %copy-done.5 = s32[2,12]{1,0:T(2,128)S(1)} copy-done((s32[2,12]{1,0:T(2,128)S(1)}, s32[2,12]{1,0:T(2,128)}, u32[]{:S(2)}) %copy-start.5) | copy-done | bytes 120
  6.5 39.4 %shard_map.77 = (f32[8,12,32,128]{3,2,1,0:T(8,128)S(1)}, f32[2,8,128]{2,1,0:T(8,128)S(1)}) custom-call(s32[2,12]{1,0:T(2,128)S(1)} %copy-done.5, bf16[8,12,32,128]{3,2,1,0:T(8,128)(2,1)S(1)} %copy-done.1, f32[12,32,128]{2,1,0:T(8,128)S(1)} %copy-done.2, s32[12,32,128]{2,1,0:T(8,128)S(1)} %copy-done.3, f32[2,32,128]{2,1,0:T(8,128)S(1)} %copy-done.4, ...), custom_call_target="tpu_custom_call" | custom-call | tf_op jit(solution)/shard_map/pallas_call | solution.py:317
  45.9 0.5 %fusion = (f32[1,1,1]{2,1,0:T(1,128)}, f32[1,1,1]{2,1,0:T(1,128)}) fusion(f32[2,8,128]{2,1,0:T(8,128)S(1)} %get-tuple-element.5), kind=kLoop, calls=%fused_computation.1 | loop fusion | bytes 16 | tf_op jit(solution)/shard_map/slice | solution.py:359
  46.4 1.9 %broadcast_multiply_fusion = f32[8,12,32,128]{3,2,1,0:T(8,128)} fusion(f32[8,12,32,128]{3,2,1,0:T(8,128)S(1)} %get-tuple-element.4, f32[]{:T(128)} %bitcast), kind=kLoop, calls=%fused_computation | loop fusion | flops 393216 | bytes 3145732 | tf_op jit(solution)/shard_map/mul | solution.py:359
Async XLA Ops:
  0.6 1.4 %copy-start = (f32[8,12,32,128]{3,2,1,0:T(8,128)S(1)}, f32[8,12,32,128]{3,2,1,0:T(8,128)}, u32[]{:S(2)}) copy-start(f32[8,12,32,128]{3,2,1,0:T(8,128)} %alpha_any.1) | copy-start | bytes 4718596
  2.0 1.1 %copy-start.1 = (bf16[8,12,32,128]{3,2,1,0:T(8,128)(2,1)S(1)}, bf16[8,12,32,128]{3,2,1,0:T(8,128)(2,1)}, u32[]{:S(2)}) copy-start(bf16[8,12,32,128]{3,2,1,0:T(8,128)(2,1)} %anom_any.1) | copy-start | bytes 2359300
  3.2 0.9 %copy-start.2 = (f32[12,32,128]{2,1,0:T(8,128)S(1)}, f32[12,32,128]{2,1,0:T(8,128)}, u32[]{:S(2)}) copy-start(f32[12,32,128]{2,1,0:T(8,128)} %gin_any.1) | copy-start | bytes 589828
  4.1 0.9 %copy-start.3 = (s32[12,32,128]{2,1,0:T(8,128)S(1)}, s32[12,32,128]{2,1,0:T(8,128)}, u32[]{:S(2)}) copy-start(s32[12,32,128]{2,1,0:T(8,128)} %land_any.1) | copy-start | bytes 589828
  5.0 0.8 %copy-start.4 = (f32[2,32,128]{2,1,0:T(8,128)S(1)}, f32[2,32,128]{2,1,0:T(8,128)}, u32[]{:S(2)}) copy-start(f32[2,32,128]{2,1,0:T(8,128)} %rate_any.1) | copy-start | bytes 98308
  5.8 0.7 %copy-start.5 = (s32[2,12]{1,0:T(2,128)S(1)}, s32[2,12]{1,0:T(2,128)}, u32[]{:S(2)}) copy-start(s32[2,12]{1,0:T(2,128)} %cnt_any.1) | copy-start | bytes 292

commit v2 on v1

--- a/solution.py
+++ b/solution.py
@@ -46,9 +46,8 @@
     ]
     for c in loads:
         c.start()
-    loads[0].wait()
-    loads[1].wait()
-    pl.semaphore_wait(barrier, ns + nm - 2)
+    for c in loads[:4]:
+        c.wait()
 
     def rdma(src, dst, ss, rs, dev):
         return pltpu.make_async_remote_copy(
@@ -83,10 +82,6 @@
     def out_copy(l):
         return pltpu.make_async_copy(g.at[:, l], proj_any.at[:, l], out_sem.at[l])
 
-    for c in coef_copies():
-        c.start()
-    loads[2].wait()
-    loads[3].wait()
 
     @pl.loop(0, levels)
     def _(l):
@@ -101,6 +96,13 @@
                     u0[l, pl.ds((16 * h + 8 * j) * nmem + m, 8, stride=nmem), :] = (
                         a[8 * j:8 * j + 8] * facs[j]
                     )
+
+    pl.semaphore_wait(barrier, ns + nm - 2)
+    for c in coef_copies():
+        c.start()
+
+    @pl.loop(0, levels)
+    def _(l):
         for c in halo_copies(u0, 0, l):
             c.start()
 

time: 48.6 us -> 48.6 us (level)
  no operation moved by 1% of the time
where the time goes in v2:
time: 48.6 us; the launch traced here: 48.2 us
  Pallas kernels  39.4 us (81%)
  local copies, waits for them, and re-layouts  6.34 us (13%)
  other arithmetic  1.87 us (4%)
  between operations  0.65 us (1%)
    pallas_call x1, Pallas kernels, on_device(): pl.pallas_call(body, out_shape=(jax.ShapeDtypeStruct(alpha.shape, f32), j...  39.4 us
    unnamed x12, local copies, waits for them, and re-layouts  5.82 us
    mul x1, other arithmetic, on_device(): return (projected * stats[1, 0, 0], stats[0, 0, 0])  1.87 us

profile of v2, /device:TPU:0, one launch (start us, length us, event | category | flops | bytes accessed | tf_op | source)
XLA Modules:
  0.0 48.2 jit_solution(11800520237548551024)
XLA Ops:
  0.6 0.0 copy-start
  0.6 1.4 %copy-done = f32[8,12,32,128]{3,2,1,0:T(8,128)S(1)} copy-done((f32[8,12,32,128]{3,2,1,0:T(8,128)S(1)}, f32[8,12,32,128]{3,2,1,0:T(8,128)}, u32[]{:S(2)}) %copy-start) | copy-done | bytes 1572888
  2.0 0.0 copy-start.1
  2.0 1.1 %copy-done.1 = bf16[8,12,32,128]{3,2,1,0:T(8,128)(2,1)S(1)} copy-done((bf16[8,12,32,128]{3,2,1,0:T(8,128)(2,1)S(1)}, bf16[8,12,32,128]{3,2,1,0:T(8,128)(2,1)}, u32[]{:S(2)}) %copy-start.1) | copy-done | bytes 786456
  3.2 0.0 copy-start.2
  3.2 0.9 %copy-done.2 = f32[12,32,128]{2,1,0:T(8,128)S(1)} copy-done((f32[12,32,128]{2,1,0:T(8,128)S(1)}, f32[12,32,128]{2,1,0:T(8,128)}, u32[]{:S(2)}) %copy-start.2) | copy-done | bytes 196632
  4.1 0.0 copy-start.3
  4.1 0.9 %copy-done.3 = s32[12,32,128]{2,1,0:T(8,128)S(1)} copy-done((s32[12,32,128]{2,1,0:T(8,128)S(1)}, s32[12,32,128]{2,1,0:T(8,128)}, u32[]{:S(2)}) %copy-start.3) | copy-done | bytes 196632
  5.0 0.0 copy-start.4
  5.0 0.8 %copy-done.4 = f32[2,32,128]{2,1,0:T(8,128)S(1)} copy-done((f32[2,32,128]{2,1,0:T(8,128)S(1)}, f32[2,32,128]{2,1,0:T(8,128)}, u32[]{:S(2)}) %copy-start.4) | copy-done | bytes 32792
  5.8 0.0 copy-start.5
  5.8 0.7 %copy-done.5 = s32[2,12]{1,0:T(2,128)S(1)} copy-done((s32[2,12]{1,0:T(2,128)S(1)}, s32[2,12]{1,0:T(2,128)}, u32[]{:S(2)}) %copy-start.5) | copy-done | bytes 120
  6.5 39.4 %shard_map.77 = (f32[8,12,32,128]{3,2,1,0:T(8,128)S(1)}, f32[2,8,128]{2,1,0:T(8,128)S(1)}) custom-call(s32[2,12]{1,0:T(2,128)S(1)} %copy-done.5, bf16[8,12,32,128]{3,2,1,0:T(8,128)(2,1)S(1)} %copy-done.1, f32[12,32,128]{2,1,0:T(8,128)S(1)} %copy-done.2, s32[12,32,128]{2,1,0:T(8,128)S(1)} %copy-done.3, f32[2,32,128]{2,1,0:T(8,128)S(1)} %copy-done.4, ...), custom_call_target="tpu_custom_call" | custom-call | tf_op jit(solution)/shard_map/pallas_call | solution.py:319
  45.9 0.5 %fusion = (f32[1,1,1]{2,1,0:T(1,128)}, f32[1,1,1]{2,1,0:T(1,128)}) fusion(f32[2,8,128]{2,1,0:T(8,128)S(1)} %get-tuple-element.5), kind=kLoop, calls=%fused_computation.1 | loop fusion | bytes 16 | tf_op jit(solution)/shard_map/slice | solution.py:361
  46.4 1.9 %broadcast_multiply_fusion = f32[8,12,32,128]{3,2,1,0:T(8,128)} fusion(f32[8,12,32,128]{3,2,1,0:T(8,128)S(1)} %get-tuple-element.4, f32[]{:T(128)} %bitcast), kind=kLoop, calls=%fused_computation | loop fusion | flops 393216 | bytes 3145732 | tf_op jit(solution)/shard_map/mul | solution.py:361
Async XLA Ops:
  0.6 1.4 %copy-start = (f32[8,12,32,128]{3,2,1,0:T(8,128)S(1)}, f32[8,12,32,128]{3,2,1,0:T(8,128)}, u32[]{:S(2)}) copy-start(f32[8,12,32,128]{3,2,1,0:T(8,128)} %alpha_any.1) | copy-start | bytes 4718596
  2.0 1.1 %copy-start.1 = (bf16[8,12,32,128]{3,2,1,0:T(8,128)(2,1)S(1)}, bf16[8,12,32,128]{3,2,1,0:T(8,128)(2,1)}, u32[]{:S(2)}) copy-start(bf16[8,12,32,128]{3,2,1,0:T(8,128)(2,1)} %anom_any.1) | copy-start | bytes 2359300
  3.2 0.9 %copy-start.2 = (f32[12,32,128]{2,1,0:T(8,128)S(1)}, f32[12,32,128]{2,1,0:T(8,128)}, u32[]{:S(2)}) copy-start(f32[12,32,128]{2,1,0:T(8,128)} %gin_any.1) | copy-start | bytes 589828
  4.1 0.9 %copy-start.3 = (s32[12,32,128]{2,1,0:T(8,128)S(1)}, s32[12,32,128]{2,1,0:T(8,128)}, u32[]{:S(2)}) copy-start(s32[12,32,128]{2,1,0:T(8,128)} %land_any.1) | copy-start | bytes 589828
  5.0 0.8 %copy-start.4 = (f32[2,32,128]{2,1,0:T(8,128)S(1)}, f32[2,32,128]{2,1,0:T(8,128)}, u32[]{:S(2)}) copy-start(f32[2,32,128]{2,1,0:T(8,128)} %rate_any.1) | copy-start | bytes 98308
  5.8 0.7 %copy-start.5 = (s32[2,12]{1,0:T(2,128)S(1)}, s32[2,12]{1,0:T(2,128)}, u32[]{:S(2)}) copy-start(s32[2,12]{1,0:T(2,128)} %cnt_any.1) | copy-start | bytes 292

commit v3 on v2

--- a/solution.py
+++ b/solution.py
@@ -10,7 +10,7 @@
 NSTEP = 8
 SURE = 6
 W = NSTEP
-GROUP = 3
+GROUP = 4
 MESH = pl.DeviceIdType.MESH
 
 

time: 48.6 us -> 48.5 us (level)
  no operation moved by 1% of the time
where the time goes in v3:
time: 48.5 us; the launch traced here: 48.2 us
  Pallas kernels  39.3 us (81%)
  local copies, waits for them, and re-layouts  6.34 us (13%)
  other arithmetic  1.87 us (4%)
  between operations  0.65 us (1%)
    pallas_call x1, Pallas kernels, on_device(): pl.pallas_call(body, out_shape=(jax.ShapeDtypeStruct(alpha.shape, f32), j...  39.3 us
    unnamed x12, local copies, waits for them, and re-layouts  5.82 us
    mul x1, other arithmetic, on_device(): return (projected * stats[1, 0, 0], stats[0, 0, 0])  1.87 us

profile of v3, /device:TPU:0, one launch (start us, length us, event | category | flops | bytes accessed | tf_op | source)
XLA Modules:
  0.0 48.2 jit_solution(13073902569498198929)
XLA Ops:
  0.6 0.0 copy-start
  0.6 1.4 %copy-done = f32[8,12,32,128]{3,2,1,0:T(8,128)S(1)} copy-done((f32[8,12,32,128]{3,2,1,0:T(8,128)S(1)}, f32[8,12,32,128]{3,2,1,0:T(8,128)}, u32[]{:S(2)}) %copy-start) | copy-done | bytes 1572888
  2.0 0.0 copy-start.1
  2.0 1.1 %copy-done.1 = bf16[8,12,32,128]{3,2,1,0:T(8,128)(2,1)S(1)} copy-done((bf16[8,12,32,128]{3,2,1,0:T(8,128)(2,1)S(1)}, bf16[8,12,32,128]{3,2,1,0:T(8,128)(2,1)}, u32[]{:S(2)}) %copy-start.1) | copy-done | bytes 786456
  3.2 0.0 copy-start.2
  3.2 0.9 %copy-done.2 = f32[12,32,128]{2,1,0:T(8,128)S(1)} copy-done((f32[12,32,128]{2,1,0:T(8,128)S(1)}, f32[12,32,128]{2,1,0:T(8,128)}, u32[]{:S(2)}) %copy-start.2) | copy-done | bytes 196632
  4.1 0.0 copy-start.3
  4.1 0.9 %copy-done.3 = s32[12,32,128]{2,1,0:T(8,128)S(1)} copy-done((s32[12,32,128]{2,1,0:T(8,128)S(1)}, s32[12,32,128]{2,1,0:T(8,128)}, u32[]{:S(2)}) %copy-start.3) | copy-done | bytes 196632
  5.0 0.0 copy-start.4
  5.0 0.8 %copy-done.4 = f32[2,32,128]{2,1,0:T(8,128)S(1)} copy-done((f32[2,32,128]{2,1,0:T(8,128)S(1)}, f32[2,32,128]{2,1,0:T(8,128)}, u32[]{:S(2)}) %copy-start.4) | copy-done | bytes 32792
  5.8 0.0 copy-start.5
  5.8 0.7 %copy-done.5 = s32[2,12]{1,0:T(2,128)S(1)} copy-done((s32[2,12]{1,0:T(2,128)S(1)}, s32[2,12]{1,0:T(2,128)}, u32[]{:S(2)}) %copy-start.5) | copy-done | bytes 120
  6.5 39.3 %shard_map.77 = (f32[8,12,32,128]{3,2,1,0:T(8,128)S(1)}, f32[2,8,128]{2,1,0:T(8,128)S(1)}) custom-call(s32[2,12]{1,0:T(2,128)S(1)} %copy-done.5, bf16[8,12,32,128]{3,2,1,0:T(8,128)(2,1)S(1)} %copy-done.1, f32[12,32,128]{2,1,0:T(8,128)S(1)} %copy-done.2, s32[12,32,128]{2,1,0:T(8,128)S(1)} %copy-done.3, f32[2,32,128]{2,1,0:T(8,128)S(1)} %copy-done.4, ...), custom_call_target="tpu_custom_call" | custom-call | tf_op jit(solution)/shard_map/pallas_call | solution.py:319
  45.8 0.5 %fusion = (f32[1,1,1]{2,1,0:T(1,128)}, f32[1,1,1]{2,1,0:T(1,128)}) fusion(f32[2,8,128]{2,1,0:T(8,128)S(1)} %get-tuple-element.5), kind=kLoop, calls=%fused_computation.1 | loop fusion | bytes 16 | tf_op jit(solution)/shard_map/slice | solution.py:361
  46.3 1.9 %broadcast_multiply_fusion = f32[8,12,32,128]{3,2,1,0:T(8,128)} fusion(f32[8,12,32,128]{3,2,1,0:T(8,128)S(1)} %get-tuple-element.4, f32[]{:T(128)} %bitcast), kind=kLoop, calls=%fused_computation | loop fusion | flops 393216 | bytes 3145732 | tf_op jit(solution)/shard_map/mul | solution.py:361
Async XLA Ops:
  0.6 1.4 %copy-start = (f32[8,12,32,128]{3,2,1,0:T(8,128)S(1)}, f32[8,12,32,128]{3,2,1,0:T(8,128)}, u32[]{:S(2)}) copy-start(f32[8,12,32,128]{3,2,1,0:T(8,128)} %alpha_any.1) | copy-start | bytes 4718596
  2.0 1.1 %copy-start.1 = (bf16[8,12,32,128]{3,2,1,0:T(8,128)(2,1)S(1)}, bf16[8,12,32,128]{3,2,1,0:T(8,128)(2,1)}, u32[]{:S(2)}) copy-start(bf16[8,12,32,128]{3,2,1,0:T(8,128)(2,1)} %anom_any.1) | copy-start | bytes 2359300
  3.2 0.9 %copy-start.2 = (f32[12,32,128]{2,1,0:T(8,128)S(1)}, f32[12,32,128]{2,1,0:T(8,128)}, u32[]{:S(2)}) copy-start(f32[12,32,128]{2,1,0:T(8,128)} %gin_any.1) | copy-start | bytes 589828
  4.1 0.9 %copy-start.3 = (s32[12,32,128]{2,1,0:T(8,128)S(1)}, s32[12,32,128]{2,1,0:T(8,128)}, u32[]{:S(2)}) copy-start(s32[12,32,128]{2,1,0:T(8,128)} %land_any.1) | copy-start | bytes 589828
  5.0 0.8 %copy-start.4 = (f32[2,32,128]{2,1,0:T(8,128)S(1)}, f32[2,32,128]{2,1,0:T(8,128)}, u32[]{:S(2)}) copy-start(f32[2,32,128]{2,1,0:T(8,128)} %rate_any.1) | copy-start | bytes 98308
  5.8 0.7 %copy-start.5 = (s32[2,12]{1,0:T(2,128)S(1)}, s32[2,12]{1,0:T(2,128)}, u32[]{:S(2)}) copy-start(s32[2,12]{1,0:T(2,128)} %cnt_any.1) | copy-start | bytes 292
